TPU v7x, 256 devices: a whole 4x4x8 slice. The times are simulated.
256 devices in a mesh: seq: 8 (over z), head: 8 (over x, core), rep: 4 (over y).
Axes of the slice: x: 4, y: 4, z: 8, core: 2. Of those that a mesh axis runs over, the one named last changes fastest.
Arguments:
- queries: bfloat16 [16384, 8192], P(('rep', 'seq', 'head')), parts along dimension 0, may hold values from -6 to 6
- keys: bfloat16 [16384, 1024], P(('rep', 'seq', 'head')), parts along dimension 0, may hold values from -4.6 to 4.6
- values: bfloat16 [16384, 1024], P(('rep', 'seq', 'head')), parts along dimension 0, may hold values from -6 to 6
- counts: int32 [256, 8], P(('rep', 'seq', 'head')), parts along dimension 0, may hold values from 0 to 32, as said below
- offsets: int32 [256, 8], P(('rep', 'seq', 'head')), parts along dimension 0, may hold values from 0 to 64, as said below
- tree_ids: int32 [256, 8], P(('rep', 'seq', 'head')), parts along dimension 0, may hold values from 0 to 3
- block_lists: int32 [32, 16, 7], P(('rep', 'seq')), parts along dimension 0, may hold values from -1 to 14, as said below
Outputs:
- attended: bfloat16 [16384, 8192], P(('rep', 'seq', 'head')), parts along dimension 0
There are 4 independent parts, one for each index of `rep`. A program takes and returns all parts, laid end to end along the dimension named above; each array names one. Nothing has to cross between parts.
Inputs may be any that keep to these rules, and one draw needn't show every extreme that they name: Each worker's counts sum to 64 and are at most 32; in every draw one shard receives exactly 32 rows from every worker. For each worker the segments [offsets, offsets + counts) over all shards tile its rows 0 to 63. Entry k of block_lists[s, b] is the (k + 1)-th nearest ancestor of block b in a tree over the blocks of shard s, each ancestor an earlier block; -1 past the root.
All inputs are finite; a program needn't handle non-finite values.
Results may differ from a plain program's by a relative error of at most 0.0024.
Values may be sent and summed in bfloat16 or wider, within the bound.
A program may use at most 64 MiB of HBM per device.

v0:
```python
import math

import jax
import jax.numpy as jnp
from jax import lax
from jax.sharding import PartitionSpec as P

QUERY_HEADS = 64
KEY_VALUE_HEADS = 8
HEAD_SIZE = 128
MASK_BLOCK_ROWS = 128
ANCESTOR_COUNT = 7
SLOT = 32


def body(queries, keys, values, counts, offsets, tree_ids, block_lists):
    seq_count = lax.axis_size("seq")
    total_heads = lax.axis_size("head")
    workers = seq_count * total_heads
    local_key_value = KEY_VALUE_HEADS // total_heads
    query_group_width = QUERY_HEADS // KEY_VALUE_HEADS
    q_width = local_key_value * query_group_width * HEAD_SIZE
    kv_width = local_key_value * HEAD_SIZE
    tok_rows = queries.shape[0]
    score_scale = 1.0 / math.sqrt(HEAD_SIZE)
    amounts = counts[0]
    starts = offsets[0]
    trees = tree_ids[0]
    slot_pos = jnp.arange(SLOT, dtype=jnp.int32)
    slot_live = slot_pos[None, :] < amounts[:, None]
    source = jnp.where(slot_live, starts[:, None] + slot_pos[None, :], 0)
    packed = jnp.concatenate(
        [
            queries.reshape(tok_rows, total_heads, q_width),
            keys.reshape(tok_rows, total_heads, kv_width),
            values.reshape(tok_rows, total_heads, kv_width),
        ],
        axis=2,
    )
    head_ids = jnp.arange(total_heads, dtype=jnp.int32)
    outgoing = packed[source[:, None, :], head_ids[None, :, None]]
    outgoing = jnp.where(slot_live[:, None, :, None], outgoing, jnp.zeros((), jnp.bfloat16))
    slot_info = jnp.broadcast_to(
        jnp.stack([amounts, trees], axis=1)[:, None, :], (seq_count, total_heads, 2)
    )
    arrived, details = (
        lax.all_to_all(
            lax.all_to_all(outgoing, "seq", split_axis=0, concat_axis=0, tiled=True),
            "head",
            split_axis=1,
            concat_axis=1,
            tiled=True,
        ),
        lax.all_to_all(
            lax.all_to_all(slot_info, "seq", split_axis=0, concat_axis=0, tiled=True),
            "head",
            split_axis=1,
            concat_axis=1,
            tiled=True,
        ),
    )
    row_count = workers * SLOT
    arrived = arrived.reshape(row_count, q_width + 2 * kv_width)
    details = details.reshape(workers, 2)
    row_live = (slot_pos[None, :] < details[:, 0:1]).reshape(row_count)
    row_tree = jnp.repeat(details[:, 1], SLOT)
    q_local = arrived[:, :q_width].reshape(row_count, local_key_value, query_group_width, HEAD_SIZE)
    k_local = arrived[:, q_width : q_width + kv_width].reshape(
        row_count, local_key_value, HEAD_SIZE
    )
    v_local = arrived[:, q_width + kv_width :].reshape(row_count, local_key_value, HEAD_SIZE)
    ancestry = block_lists[0]
    block_pos = jnp.arange(MASK_BLOCK_ROWS, dtype=jnp.int32)
    diagonal = jnp.repeat(jnp.arange(ANCESTOR_COUNT + 1) == ANCESTOR_COUNT, MASK_BLOCK_ROWS)
    causal = jnp.logical_not(diagonal)[None, :] | (
        jnp.tile(block_pos, ANCESTOR_COUNT + 1)[None, :] <= block_pos[:, None]
    )

    def attend_block(block_idx):
        key_blocks = jnp.concatenate([ancestry[block_idx], block_idx[None]])
        valid_block = key_blocks >= 0
        key_row_values = (
            jnp.maximum(key_blocks, 0)[:, None] * MASK_BLOCK_ROWS + block_pos[None, :]
        ).reshape(-1)
        query_row_values = block_idx * MASK_BLOCK_ROWS + block_pos
        key_ok = jnp.repeat(valid_block, MASK_BLOCK_ROWS) & row_live[key_row_values]
        same_tree = row_tree[query_row_values][:, None] == row_tree[key_row_values][None, :]
        allowed = key_ok[None, :] & same_tree & causal
        query_block_tile = lax.dynamic_slice_in_dim(
            q_local, block_idx * MASK_BLOCK_ROWS, MASK_BLOCK_ROWS, 0
        )
        key_block_tile = k_local[key_row_values]
        value_block_tile = v_local[key_row_values]
        scores = (
            jnp.einsum(
                "qhgd,khd->hgqk",
                query_block_tile,
                key_block_tile,
                preferred_element_type=jnp.float32,
            )
            * score_scale
        )
        scores = jnp.where(allowed[None, None], scores, jnp.float32(-1e30))
        row_max = jnp.max(scores, axis=-1, keepdims=True)
        weights = jnp.exp(scores - row_max)
        totals = jnp.sum(weights, axis=-1)
        rounded = weights.astype(jnp.bfloat16)
        blended = (
            jnp.einsum(
                "hgqk,khd->qhgd", rounded, value_block_tile, preferred_element_type=jnp.float32
            )
            / jnp.transpose(totals, (2, 0, 1))[..., None]
        )
        return blended.reshape(MASK_BLOCK_ROWS, q_width).astype(jnp.bfloat16)

    results = lax.map(attend_block, jnp.arange(row_count // MASK_BLOCK_ROWS, dtype=jnp.int32))
    answer = results.reshape(workers, SLOT, q_width)
    returned = lax.all_to_all(
        lax.all_to_all(
            answer.reshape(seq_count, total_heads, SLOT, q_width),
            "seq",
            split_axis=0,
            concat_axis=0,
            tiled=True,
        ),
        "head",
        split_axis=1,
        concat_axis=1,
        tiled=True,
    )
    positions = jnp.arange(tok_rows, dtype=jnp.int32)
    member = (
        (starts[None, :] <= positions[:, None]) & (positions[:, None] < (starts + amounts)[None, :])
    ).astype(jnp.int32)
    segment = jnp.sum(member * jnp.arange(seq_count, dtype=jnp.int32)[None, :], axis=1)
    within = positions - jnp.sum(member * starts[None, :], axis=1)
    gathered = returned[segment[:, None], head_ids[None, :], within[:, None]]
    return gathered.reshape(tok_rows, QUERY_HEADS * HEAD_SIZE)


def solution(mesh):
    placed = (
        P(("rep", "seq", "head"), None),
        P(("rep", "seq", "head"), None),
        P(("rep", "seq", "head"), None),
        P(("rep", "seq", "head"), None),
        P(("rep", "seq", "head"), None),
        P(("rep", "seq", "head"), None),
        P(("rep", "seq"), None, None),
    )
    return jax.shard_map(
        body, mesh=mesh, in_specs=placed, out_specs=P(("rep", "seq", "head"), None), check_vma=False
    )
```

profile of v0, /device:TPU:235, one launch (start us, length us, event | category | flops | bytes accessed | tf_op | source)
XLA Modules:
  0.0 992.3 jit_solution(6889717602797219035)
XLA Ops:
  12.1 33.7 %gather_fusion.5 = bf16[2048,1280]{1,0:T(8,128)(2,1)} fusion(bf16[64,8,1280]{2,1,0:T(8,128)(2,1)S(1)} %pad_maximum_fusion, s32[2048]{0:T(1024)S(1)} %reshape.349), kind=kCustom, calls=%fused_computation.5 | custom fusion | bytes 10502144 | tf_op jit(solution)/shard_map/gather | solution.py:41
  58.3 106.4 %all-to-all-done = bf16[8,8,32,1280]{3,2,1,0:T(8,128)(2,1)} async-done(((bf16[8,8,32,1280]{3,2,1,0:T(8,128)(2,1)}), bf16[8,8,32,1280]{3,2,1,0:T(8,128)(2,1)}, u32[]{:S(2)}, u32[]{:S(2)}) %all-to-all-start) | async-done | bytes 5242912 | tf_op jit(solution)/shard_map/all_to_all | solution.py:48
  164.7 8.0 all-to-all-start.3
  183.2 58.7 %all-to-all-done.1 = bf16[8,8,32,1280]{3,2,0,1:T(8,128)(2,1)} async-done(((bf16[8,8,32,1280]{3,2,0,1:T(8,128)(2,1)}), bf16[8,8,32,1280]{3,2,0,1:T(8,128)(2,1)}, u32[]{:S(2)}, u32[]{:S(2)}) %all-to-all-start.1) | async-done | bytes 5242912 | tf_op jit(solution)/shard_map/all_to_all | solution.py:47
  254.1 563.8 %while.12 = (s32[]{:T(128)}, bf16[16,128,1024]{2,1,0:T(8,128)(2,1)}, s32[16]{0:T(128)S(1)}, s32[16,7]{1,0:T(8,128)S(1)}, bf16[2048,1,128]{2,0,1:T(8,128)(2,1)S(1...) while((s32[]{:T(128)}, ...), condition=%wide.region_3.4_spmd.clone.clone, body=%wide.region_0.3_spmd.clone.clone.sunk | while | flops 549330496 | bytes 33149408 | solution.py:116
  257.5 6.8 gather_fusion.2
  292.8 6.8 gather_fusion.2
  328.0 6.8 gather_fusion.2
  363.2 6.8 gather_fusion.2
  398.5 6.8 gather_fusion.2
  433.7 6.8 gather_fusion.2
  469.0 6.8 gather_fusion.2
  504.2 6.8 gather_fusion.2
  539.4 6.8 gather_fusion.2
  574.7 6.8 gather_fusion.2
  609.9 6.8 gather_fusion.2
  645.2 6.8 gather_fusion.2
  680.4 6.8 gather_fusion.2
  715.6 6.8 gather_fusion.2
  786.1 6.8 gather_fusion.2
  817.9 102.1 %all_to_all.30 = bf16[8,8,32,1024]{3,2,1,0:T(8,128)(2,1)S(1)} all-to-all(bf16[8,8,32,1024]{3,2,1,0:T(8,128)(2,1)} %bitcast.151), channel_id=1, replica_groups=mesh['seq'=8,'head'=8,'rep'=4] {'seq'}, dimensions={0} | all-to-all | bytes 8388608 | tf_op jit(solution)/shard_map/all_to_all | solution.py:119
  922.4 8.8 all-to-all-start.5
  931.6 47.5 %all-to-all-done.5 = bf16[8,8,32,1024]{3,2,0,1:T(8,128)(2,1)} async-done(((bf16[8,8,32,1024]{3,2,0,1:T(8,128)(2,1)}), bf16[8,8,32,1024]{3,2,0,1:T(8,128)(2,1)}, u32[]{:S(2)}, u32[]{:S(2)}) %all-to-all-start.5) | async-done | bytes 4194336 | tf_op jit(solution)/shard_map/all_to_all | solution.py:118
  984.1 6.9 gather_fusion.6
  (464 shorter events, 476.4 us)
Async XLA Ops:
  1.4 49.6 %all-to-all-start.2 = ((s32[8,8,2]{1,2,0:T(2,128)}), s32[8,8,2]{1,2,0:T(2,128)S(1)}, u32[]{:S(2)}, u32[]{:S(2)}) async-start(s32[8,8,2]{1,2,0:T(2,128)} %broadcast_in_dim.71), calls=%async_computation.2 | async-start | bytes 16384 | tf_op jit(solution)/shard_map/all_to_all | solution.py:55
  51.0 113.7 %all-to-all-start = ((bf16[8,8,32,1280]{3,2,1,0:T(8,128)(2,1)}), bf16[8,8,32,1280]{3,2,1,0:T(8,128)(2,1)}, u32[]{:S(2)}, u32[]{:S(2)}) async-start(bf16[8,8,32,1280]{3,2,1,0:T(8,128)(2,1)} %broadcast_select_fusion), calls=%async_computation | async-start | bytes 10485760 | tf_op jit(solution)/shard_map/all_to_all | solution.py:48
  164.7 13.2 %all-to-all-start.3 = ((s32[8,8,2]{0,2,1:T(2,128)}), s32[8,8,2]{0,2,1:T(2,128)S(1)}, u32[]{:S(2)}, u32[]{:S(2)}) async-start(s32[8,8,2]{0,2,1:T(2,128)} %copy.82), calls=%async_computation.3 | async-start | bytes 16384 | tf_op jit(solution)/shard_map/all_to_all | solution.py:54
  178.0 4.9 copy-start.1
  178.0 64.0 %all-to-all-start.1 = ((bf16[8,8,32,1280]{3,2,0,1:T(8,128)(2,1)}), bf16[8,8,32,1280]{3,2,0,1:T(8,128)(2,1)}, u32[]{:S(2)}, u32[]{:S(2)}) async-start(bf16[8,8,32,1280]{3,2,0,1:T(8,128)(2,1)} %copy.78), calls=%async_computation.1 | async-start | bytes 10485760 | tf_op jit(solution)/shard_map/all_to_all | solution.py:47
  279.1 2.0 copy-start
  314.3 2.0 copy-start
  349.6 2.0 copy-start
  384.8 2.0 copy-start
  420.0 2.0 copy-start
  455.3 2.0 copy-start
  490.5 2.0 copy-start
  525.7 2.0 copy-start
  561.0 2.0 copy-start
  596.2 2.0 copy-start
  631.5 2.0 copy-start
  666.7 2.0 copy-start
  702.0 2.0 copy-start
  737.2 2.0 copy-start
  772.4 2.0 copy-start
  807.7 2.0 copy-start
  922.4 8.8 copy-start.2
  922.4 8.8 copy-start.3
  922.4 56.6 %all-to-all-start.5 = ((bf16[8,8,32,1024]{3,2,0,1:T(8,128)(2,1)}), bf16[8,8,32,1024]{3,2,0,1:T(8,128)(2,1)}, u32[]{:S(2)}, u32[]{:S(2)}) async-start(bf16[8,8,32,1024]{3,2,0,1:T(8,128)(2,1)} %copy.87), calls=%async_computation.5 | async-start | bytes 8388608 | tf_op jit(solution)/shard_map/all_to_all | solution.py:118
where the time goes:
time: 1000 us; the launch traced here: 992 us
  local copies, waits for them, and re-layouts  460 us (46%)
  waiting for transfers between devices  213 us (21%)
  blocking collectives  102 us (10%)
  matrix products  79.6 us (8%)
  other arithmetic  62.9 us (6%)
  loops' own time  41.6 us (4%)
  starting transfers between devices  33.7 us (3%)
    gather x16, local copies, waits for them, and re-layouts, attend_block(): key_ok = jnp.repeat(valid_block, MASK_BLOCK_ROWS) & row_live[key_row_values]  109 us
    all_to_all x1, waiting for transfers between devices, body(): lax.all_to_all(outgoing, 'seq', split_axis=0, concat_axis=0, tiled=True)  106 us
    all_to_all x1, blocking collectives, body(): lax.all_to_all(answer.reshape(seq_count, total_heads, SLOT, q_width), 'se...  102 us
    gather x16, local copies, waits for them, and re-layouts, attend_block(): row_tree[key_row_values][None, :]  98.4 us
    all_to_all x1, waiting for transfers between devices, body(): lax.all_to_all(lax.all_to_all(outgoing, 'seq', split_axis=0, concat_axis=...  58.7 us
    dot_general x16, matrix products, attend_block(): jnp.einsum('hgqk,khd->qhgd', rounded, value_block_tile, preferred_element...  52.7 us
    gather x16, local copies, waits for them, and re-layouts, attend_block(): value_block_tile = v_local[key_row_values]  51.3 us
    gather x16, local copies, waits for them, and re-layouts, attend_block(): key_block_tile = k_local[key_row_values]  51.3 us
  transfers between devices with their start and end apart: 5, of which 3 were waited for; matrix products, arithmetic and copies ran while one was open for 5% of the time, Pallas kernels for 0%

commit v1 on v0

v1 whole, which is shorter than its diff:
```python
import math

import jax
import jax.numpy as jnp
from jax import lax
from jax.experimental import pallas as pl
from jax.experimental.pallas import tpu as pltpu
from jax.sharding import PartitionSpec as P

MESH = pl.DeviceIdType.MESH
KEY_VALUE_HEADS = 8
GROUP = 8
HEAD_SIZE = 128
TOK_W = 64
ANCESTOR_COUNT = 7
QB = 16
N_SEQ = 8
N_HEAD = 8
ROW = N_HEAD * TOK_W
WIDE = GROUP * HEAD_SIZE
QROWS = GROUP * TOK_W
NEG = -1e30
FACTOR = math.log2(math.e) / math.sqrt(HEAD_SIZE)
NT = (((1,), (1,)), ((), ()))


def kernel(
    cnt_ref, off_ref, tree_ref, bl_ref, q_ref, k_ref, v_ref, out_ref,
    qbuf, kv, feat, ids, anc, qa, sbuf, mx, den, acc, stage,
    own_sem, kv_s, kv_r, id_s, id_r, q_s, q_r, ring_s, ring_r, idr_s, idr_r, an_s, an_r, o_s, o_r,
):
    z = lax.axis_index("seq")
    h = lax.axis_index("head")
    up = lax.rem(z + 1, N_SEQ)
    down = lax.rem(z + N_SEQ - 1, N_SEQ)

    barrier = pltpu.get_barrier_semaphore()
    for d in range(1, N_HEAD):
        pl.semaphore_signal(barrier, inc=1, device_id={"head": lax.rem(h + d, N_HEAD)}, device_id_type=MESH)
    pl.semaphore_signal(barrier, inc=1, device_id={"seq": up}, device_id_type=MESH)
    pl.semaphore_signal(barrier, inc=1, device_id={"seq": down}, device_id_type=MESH)

    lane1 = lax.broadcasted_iota(jnp.int32, (1, 128), 1)
    cls = jnp.zeros((1, 128), jnp.float32)
    for s in range(N_SEQ):
        start = off_ref[0, s]
        member = (lane1 >= start) & (lane1 < start + cnt_ref[0, s])
        cls = jnp.where(member, (s * 4 + tree_ref[0, s]).astype(jnp.float32), cls)
    ids[z, h] = cls
    lane_block = (lane1 - 32) >> 2
    for b in range(QB):
        hit = jnp.zeros((1, 128), jnp.float32)
        for k in range(ANCESTOR_COUNT):
            e = bl_ref[0, b, k]
            hit = jnp.where((lane_block == e) & (lane1 >= 32), 1.0, hit)
        anc[z, b] = hit

    def cols(p):
        return pl.ds(pl.multiple_of(p * HEAD_SIZE, HEAD_SIZE), HEAD_SIZE)

    def wide(p):
        return pl.ds(pl.multiple_of(p * WIDE, WIDE), WIDE)

    mine = pl.ds(pl.multiple_of(z * ROW + h * TOK_W, TOK_W), TOK_W)
    left, right = pl.ds(0, HEAD_SIZE), pl.ds(HEAD_SIZE, HEAD_SIZE)
    own = [
        pltpu.make_async_copy(k_ref.at[:, cols(h)], kv.at[mine, left], own_sem.at[0]),
        pltpu.make_async_copy(v_ref.at[:, cols(h)], kv.at[mine, right], own_sem.at[1]),
        pltpu.make_async_copy(q_ref.at[:, wide(h)], qbuf.at[h], own_sem.at[2]),
    ]
    for c in own:
        c.start()

    pl.semaphore_wait(barrier, N_HEAD + 1)

    def remote(src, dst, s_sem, r_sem, **where):
        return pltpu.make_async_remote_copy(
            src_ref=src, dst_ref=dst, send_sem=s_sem, recv_sem=r_sem, device_id=where, device_id_type=MESH
        )

    first = []
    for d in range(1, N_HEAD):
        p = lax.rem(h + d, N_HEAD)
        first.append(remote(k_ref.at[:, cols(p)], kv.at[mine, left], kv_s.at[d, 0], kv_r.at[d, 0], head=p))
        first.append(remote(v_ref.at[:, cols(p)], kv.at[mine, right], kv_s.at[d, 1], kv_r.at[d, 1], head=p))
        first.append(remote(ids.at[z, h], ids.at[z, h], id_s.at[d], id_r.at[d], head=p))
    for c in first:
        c.start()
    own[0].wait()
    own[1].wait()
    for c in first:
        c.wait_recv()

    half = ROW // 2

    def rows(r, j):
        return pl.ds(pl.multiple_of(r * ROW + j * half, half), half)

    def step(way, t):
        src = lax.rem(z + N_SEQ - t, N_SEQ) if way == 0 else lax.rem(z + t, N_SEQ)
        to = up if way == 0 else down
        halves = (0, 1) if t < 3 else (way,)
        out = [
            remote(kv.at[rows(src, j)], kv.at[rows(src, j)], ring_s.at[way, t, j], ring_r.at[way, t, j], seq=to)
            for j in halves
        ]
        if t < 3 or way == 0:
            out.append(remote(ids.at[src], ids.at[src], idr_s.at[way, t], idr_r.at[way, t], seq=to))
            out.append(remote(anc.at[src], anc.at[src], an_s.at[way, t], an_r.at[way, t], seq=to))
        return out

    steps = [[step(way, t) for t in range(4)] for way in range(2)]
    for way in range(2):
        for c in steps[way][0]:
            c.start()
    queries = [
        remote(
            q_ref.at[:, wide(lax.rem(h + d, N_HEAD))], qbuf.at[h], q_s.at[d], q_r.at[d], head=lax.rem(h + d, N_HEAD)
        )
        for d in range(1, N_HEAD)
    ]
    for c in queries:
        c.start()
    for t in range(1, 5):
        for i in range(4):
            for way in range(2):
                if i < len(steps[way][t - 1]):
                    steps[way][t - 1][i].wait_recv()
                    if t < 4:
                        if t < 3:
                            steps[way][t][i].start()
                        elif way == 0 and i != 1:
                            steps[way][t][(0, 0, 1, 2)[i]].start()
                        elif way == 1 and i == 1:
                            steps[way][t][0].start()
    own[2].wait()
    for c in queries:
        c.wait_recv()

    lane = lax.broadcasted_iota(jnp.int32, (TOK_W, 128), 1)
    tok = lax.broadcasted_iota(jnp.int32, (TOK_W, 128), 0)

    def column(row):
        return jnp.sum(jnp.where(lane == tok, row, 0.0), axis=1, keepdims=True)

    def key_features(w, carry):
        c = column(ids[w // N_HEAD, lax.rem(w, N_HEAD)])
        hot = (lane.astype(jnp.float32) == c) | (lane == 32 + w)
        feat[pl.ds(pl.multiple_of(w * TOK_W, TOK_W), TOK_W), :] = jnp.where(hot, 1.0, 0.0).astype(jnp.bfloat16)
        return carry

    lax.fori_loop(0, (z + 1) * N_HEAD, key_features, 0)

    row_id = lax.broadcasted_iota(jnp.int32, (QROWS, ROW), 0)
    col_id = lax.broadcasted_iota(jnp.int32, (QROWS, ROW), 1)

    def tile(d, carry):
        p = lax.rem(h + d, N_HEAD)
        w = z * N_HEAD + p
        b = w // 4
        c = column(ids[z, p])
        shard = jnp.floor(c * 0.25)
        looks = jnp.zeros((TOK_W, 128), jnp.float32)
        for s in range(N_SEQ):
            looks = jnp.where(shard == float(s), anc[s, b], looks)
        worker = lane - 32
        own_block = ((worker >> 2) == b) & (worker <= w)
        fine = jnp.where(
            lane < 32,
            jnp.where(lane.astype(jnp.float32) == c, 1.0, 0.0),
            jnp.where((lane >= 96) | own_block, 1.0, looks),
        )
        penalty = jnp.where(fine > 0.5, 0.0, NEG).astype(jnp.bfloat16)
        for g in range(GROUP):
            r = pl.ds(g * TOK_W, TOK_W)
            qa[r, 0:HEAD_SIZE] = qbuf[p, :, g * HEAD_SIZE : (g + 1) * HEAD_SIZE]
            qa[r, HEAD_SIZE:] = penalty

        def chunk_rows(i):
            return pl.ds(pl.multiple_of(i * ROW, ROW), ROW)

        def scores(i):
            keys = jnp.concatenate([kv[chunk_rows(i), 0:HEAD_SIZE], feat[chunk_rows(i), :]], axis=1)
            return lax.dot_general(qa[...], keys, NT, preferred_element_type=jnp.float32)

        def fold(x, op):
            return op(op(x[:, 0:128], x[:, 128:256]), op(x[:, 256:384], x[:, 384:512]))

        s = scores(z)
        late = ((col_id >> 6) == p) & ((col_id & 63) > (row_id & 63))
        s = jnp.where(late, NEG, s)
        sbuf[z] = s
        mx[...] = fold(s, jnp.maximum)

        def find(i, carry):
            s = scores(i)
            sbuf[i] = s
            mx[...] = jnp.maximum(mx[...], fold(s, jnp.maximum))
            return carry

        lax.fori_loop(0, z, find, 0)
        top = jnp.max(mx[...], axis=1, keepdims=True)
        mx[...] = jnp.broadcast_to(top, (QROWS, 128))
        den[...] = jnp.zeros_like(den)
        acc[...] = jnp.zeros_like(acc)

        def blend(i, carry):
            weights = jnp.exp2((sbuf[i] - mx[:, 0:1]) * FACTOR)
            den[...] += fold(weights, jnp.add)
            acc[...] += jnp.dot(
                weights.astype(jnp.bfloat16), kv[chunk_rows(i), HEAD_SIZE:], preferred_element_type=jnp.float32
            )
            return carry

        lax.fori_loop(0, z + 1, blend, 0)
        total = jnp.sum(den[...], axis=1, keepdims=True)
        done = (acc[...] / total).astype(jnp.bfloat16)
        for g in range(GROUP):
            stage[p, :, g * HEAD_SIZE : (g + 1) * HEAD_SIZE] = done[g * TOK_W : (g + 1) * TOK_W, :]

        @pl.when(d < N_HEAD)
        def _():
            remote(stage.at[p], out_ref.at[:, wide(h)], o_s.at[d], o_r.at[d], head=p).start()

        return carry

    lax.fori_loop(1, N_HEAD + 1, tile, 0)
    last = pltpu.make_async_copy(stage.at[h], out_ref.at[:, wide(h)], own_sem.at[0])
    last.start()
    last.wait()
    for c in first + queries:
        c.wait_send()
    for way in range(2):
        for t in range(4):
            for c in steps[way][t]:
                c.wait_send()
    for d in range(1, N_HEAD):
        p = lax.rem(h + d, N_HEAD)
        remote(stage.at[p], out_ref.at[:, wide(h)], o_s.at[d], o_r.at[d], head=p).wait()


def body(queries, keys, values, counts, offsets, tree_ids, block_lists):
    any_space = pl.BlockSpec(memory_space=pl.ANY)
    smem = pl.BlockSpec(memory_space=pltpu.SMEM)
    dma = pltpu.SemaphoreType.DMA
    return pl.pallas_call(
        kernel,
        out_shape=jax.ShapeDtypeStruct((TOK_W, KEY_VALUE_HEADS * WIDE), jnp.bfloat16),
        in_specs=[smem] * 4 + [any_space] * 3,
        out_specs=any_space,
        scratch_shapes=[
            pltpu.VMEM((N_HEAD, TOK_W, WIDE), jnp.bfloat16),
            pltpu.VMEM((N_SEQ * ROW, 2 * HEAD_SIZE), jnp.bfloat16),
            pltpu.VMEM((N_SEQ * ROW, 128), jnp.bfloat16),
            pltpu.VMEM((N_SEQ, N_HEAD, 1, 128), jnp.float32),
            pltpu.VMEM((N_SEQ, QB, 1, 128), jnp.float32),
            pltpu.VMEM((QROWS, 2 * HEAD_SIZE), jnp.bfloat16),
            pltpu.VMEM((N_SEQ, QROWS, ROW), jnp.float32),
            pltpu.VMEM((QROWS, 128), jnp.float32),
            pltpu.VMEM((QROWS, 128), jnp.float32),
            pltpu.VMEM((QROWS, HEAD_SIZE), jnp.float32),
            pltpu.VMEM((N_HEAD, TOK_W, WIDE), jnp.bfloat16),
            dma((3,)),
            dma((N_HEAD, 2)),
            dma((N_HEAD, 2)),
            dma((N_HEAD,)),
            dma((N_HEAD,)),
            dma((N_HEAD,)),
            dma((N_HEAD,)),
            dma((2, 4, 2)),
            dma((2, 4, 2)),
            dma((2, 4)),
            dma((2, 4)),
            dma((2, 4)),
            dma((2, 4)),
            dma((N_HEAD + 1,)),
            dma((N_HEAD + 1,)),
        ],
        compiler_params=pltpu.CompilerParams(
            collective_id=0, has_side_effects=True, vmem_limit_bytes=48 * 1024 * 1024
        ),
    )(counts, offsets, tree_ids, block_lists, queries, keys, values)


def solution(mesh):
    split = P(("rep", "seq", "head"), None)
    placed = (split,) * 6 + (P(("rep", "seq"), None, None),)
    return jax.shard_map(body, mesh=mesh, in_specs=placed, out_specs=split, check_vma=False)
```

time: 1000 us -> 96.8 us (0.10)
  the two profiles are of different devices: /device:TPU:235 before, /device:TPU:240 now
where the time goes in v1:
time: 96.8 us; the launch traced here: 96.7 us
  Pallas kernels  91.8 us (95%)
  local copies, waits for them, and re-layouts  4.81 us (5%)
    pallas_call x1, Pallas kernels, body(): pl.pallas_call(kernel, out_shape=jax.ShapeDtypeStruct((TOK_W, KEY_VALUE_H...  91.8 us
    unnamed x14, local copies, waits for them, and re-layouts  4.81 us

profile of v1, /device:TPU:240, one launch (start us, length us, event | category | flops | bytes accessed | tf_op | source)
XLA Modules:
  0.0 96.7 jit_solution(9755949197475622920)
XLA Ops:
  0.0 0.0 copy-start.5
  0.0 0.0 copy-start.4
  0.0 0.0 copy-start.3
  0.0 0.8 copy.8.bl_ref
  0.8 0.0 copy-done.5
  0.8 0.0 copy-done.4
  0.8 0.0 copy-done.3
  0.8 0.0 copy-start
  0.8 1.2 %copy-done = bf16[64,8192]{1,0:T(8,128)(2,1)S(1)} copy-done((bf16[64,8192]{1,0:T(8,128)(2,1)S(1)}, bf16[64,8192]{1,0:T(8,128)(2,1)}, u32[]{:S(2)}) %copy-start) | copy-done | bytes 1048600
  2.0 0.0 copy-start.1
  2.0 0.9 copy-done.1
  3.0 0.0 copy-start.2
  3.0 0.9 copy-done.2
  3.9 91.8 %shard_map.73 = bf16[64,8192]{1,0:T(8,128)(2,1)S(1)} custom-call(s32[1,8]{1,0:T(1,128)S(1)} %copy-done.3, s32[1,8]{1,0:T(1,128)S(1)} %copy-done.4, s32[1,8]{1,0:T(1,128)S(1)} %copy-done.5, s32[1,16,7]{2,1,0:T(8,128)S(1)} %copy.8.bl_ref, bf16[64,8192]{1,0:T(8,128)(2,1)S(1)} %copy-done, bf16[64,1024]{1,0:T(8,128)(2,1)S(1)} %copy-done.1, ...), custom_call_target="tpu_custom_call" | custom-call | tf_op jit(solution)/shard_map/pallas_call | solution.py:246
  95.7 1.0 %copy.10 = bf16[64,8192]{1,0:T(8,128)(2,1)} copy(bf16[64,8192]{1,0:T(8,128)(2,1)S(1)} %shard_map.73) | data formatting | bytes 2097152
Async XLA Ops:
  0.0 0.8 copy-start.5
  0.0 0.8 copy-start.4
  0.0 0.8 copy-start.3
  0.8 1.2 %copy-start = (bf16[64,8192]{1,0:T(8,128)(2,1)S(1)}, bf16[64,8192]{1,0:T(8,128)(2,1)}, u32[]{:S(2)}) copy-start(bf16[64,8192]{1,0:T(8,128)(2,1)} %q_ref.1) | copy-start | bytes 3145732
  2.0 0.9 copy-start.1
  3.0 0.9 copy-start.2

commit v2 on v1

v2 whole, which is shorter than its diff:
```python
import math

import jax
import jax.numpy as jnp
from jax import lax
from jax.experimental import pallas as pl
from jax.experimental.pallas import tpu as pltpu
from jax.sharding import PartitionSpec as P

MESH = pl.DeviceIdType.MESH
KEY_VALUE_HEADS = 8
GROUP = 8
HEAD_SIZE = 128
TOK_W = 64
SLOT = 32
ANCESTOR_COUNT = 7
QB = 16
N_SEQ = 8
N_HEAD = 8
ROW = N_HEAD * TOK_W
HALF = ROW // 2
WIDE = GROUP * HEAD_SIZE
TILE = GROUP * SLOT
QROWS = N_HEAD * TILE
PIECE = 2 * TOK_W
ORDER = (0, 1, 3, 2)
NEG = -1e30
FACTOR = math.log2(math.e) / math.sqrt(HEAD_SIZE)
NT = (((1,), (1,)), ((), ()))
BF16 = jnp.bfloat16
F32 = jnp.float32


def kernel(
    cnt_ref, off_ref, tree_ref, bl_ref, q_ref, k_ref, v_ref, out_ref,
    qbuf, kv, ks, vs, ids, anc, qa, sbuf, mx, den, acc, osort, stage,
    own_sem, kv_s, kv_r, id_s, id_r, q_s, q_r, ring_s, ring_r, idr_s, idr_r, an_s, an_r, o_s, o_r,
):
    z = lax.axis_index("seq")
    h = lax.axis_index("head")
    up = lax.rem(z + 1, N_SEQ)
    down = lax.rem(z + N_SEQ - 1, N_SEQ)

    barrier = pltpu.get_barrier_semaphore()
    for d in range(1, N_HEAD):
        pl.semaphore_signal(barrier, inc=1, device_id={"head": lax.rem(h + d, N_HEAD)}, device_id_type=MESH)
    for d in range(1, N_SEQ):
        pl.semaphore_signal(barrier, inc=1, device_id={"seq": lax.rem(z + d, N_SEQ)}, device_id_type=MESH)

    def cols(p):
        return pl.ds(pl.multiple_of(p * HEAD_SIZE, HEAD_SIZE), HEAD_SIZE)

    def wide(p):
        return pl.ds(pl.multiple_of(p * WIDE, WIDE), WIDE)

    mine = pl.ds(pl.multiple_of(z * ROW + h * TOK_W, TOK_W), TOK_W)
    left, right = pl.ds(0, HEAD_SIZE), pl.ds(HEAD_SIZE, HEAD_SIZE)
    own = [
        pltpu.make_async_copy(k_ref.at[:, cols(h)], kv.at[mine, left], own_sem.at[0]),
        pltpu.make_async_copy(v_ref.at[:, cols(h)], kv.at[mine, right], own_sem.at[1]),
        pltpu.make_async_copy(q_ref.at[:, wide(h)], qbuf.at[h], own_sem.at[2]),
    ]
    for c in own:
        c.start()

    lane1 = lax.broadcasted_iota(jnp.int32, (1, 128), 1)
    info = jnp.zeros((1, 128), F32)
    for s in range(N_SEQ):
        start, count = off_ref[0, s], cnt_ref[0, s]
        member = (lane1 >= start) & (lane1 < start + count)
        info = jnp.where(member, (s * 4 + tree_ref[0, s]).astype(F32), info)
        info = jnp.where(lane1 == TOK_W + s, count.astype(F32), info)
        info = jnp.where(lane1 == TOK_W + N_SEQ + s, start.astype(F32), info)
    ids[z, h] = info
    lane_block = (lane1 - 32) >> 2
    for b in range(QB):
        hit = jnp.zeros((1, 128), F32)
        for k in range(ANCESTOR_COUNT):
            e = bl_ref[k, 0, b]
            hit = jnp.where((lane_block == e) & (lane1 >= 32), 1.0, hit)
        anc[z, b] = hit

    pl.semaphore_wait(barrier, N_HEAD + N_SEQ - 2)

    def remote(src, dst, s_sem, r_sem, **where):
        return pltpu.make_async_remote_copy(
            src_ref=src, dst_ref=dst, send_sem=s_sem, recv_sem=r_sem, device_id=where, device_id_type=MESH
        )

    others = [lax.rem(h + d, N_HEAD) for d in range(N_HEAD)]
    id_row = [remote(ids.at[z, h], ids.at[z, h], id_s.at[d], id_r.at[d], head=others[d]) for d in range(1, N_HEAD)]
    k_row = [
        remote(k_ref.at[:, cols(others[d])], kv.at[mine, left], kv_s.at[d, 0], kv_r.at[d, 0], head=others[d])
        for d in range(1, N_HEAD)
    ]
    v_row = [
        remote(v_ref.at[:, cols(others[d])], kv.at[mine, right], kv_s.at[d, 1], kv_r.at[d, 1], head=others[d])
        for d in range(1, N_HEAD)
    ]
    q_row = [
        remote(q_ref.at[:, wide(others[d])], qbuf.at[h], q_s.at[d], q_r.at[d], head=others[d])
        for d in range(1, N_HEAD)
    ]
    for c in id_row:
        c.start()
    for a, b in zip(k_row, v_row):
        a.start()
        b.start()

    chip = h // 2

    def piece(r, j):
        c = lax.rem(chip + ORDER[j], 4)
        return kv.at[pl.ds(pl.multiple_of(r * ROW + c * PIECE, PIECE), PIECE)]

    def source(way, t):
        return lax.rem(z + N_SEQ - t, N_SEQ) if way == 0 else lax.rem(z + t, N_SEQ)

    def hop(way, t, j):
        ref = piece(source(way, t), j)
        return remote(ref, ref, ring_s.at[way, t, j], ring_r.at[way, t, j], seq=up if way == 0 else down)

    def pieces(way, t):
        return range(4) if t < 3 else (range(2) if way == 0 else range(2, 4))

    ring = {(way, t, j): hop(way, t, j) for way in range(2) for t in range(4) for j in pieces(way, t)}

    def landed(j):
        for q in range(2):
            src = lax.rem(chip + ORDER[j], 4) * 2 + q
            d = lax.rem(h + N_HEAD - src, N_HEAD)

            @pl.when(d == 0)
            def _():
                own[0].wait()
                own[1].wait()

            @pl.when(d != 0)
            def _():
                remote(kv.at[mine, left], kv.at[mine, left], kv_s.at[d, 0], kv_r.at[d, 0], head=src).wait_recv()
                remote(kv.at[mine, right], kv.at[mine, right], kv_s.at[d, 1], kv_r.at[d, 1], head=src).wait_recv()

    for j in range(4):
        landed(j)
        for way in range(2):
            ring[way, 0, j].start()
        if j == 0:
            for c in q_row:
                c.start()
        if j == 1:
            for c in id_row:
                c.wait_recv()
            id_col, an_col = [], []
            for e in range(1, N_SEQ):
                to = lax.rem(z + e, N_SEQ)
                id_col.append(remote(ids.at[z], ids.at[z], idr_s.at[e], idr_r.at[e], seq=to))
                two = pl.ds(2 * to, 2)
                an_col.append(remote(anc.at[z, two], anc.at[z, two], an_s.at[e], an_r.at[e], seq=to))
            for c in id_col + an_col:
                c.start()

    for c in id_col + an_col:
        c.wait_recv()
    least = jnp.full((1, 128), 1e9, F32)
    for r in range(N_SEQ):
        for w in range(N_HEAD):
            least = jnp.minimum(least, ids[r, w])
    lane1f = lane1.astype(F32)
    is_full = (lane1 >= TOK_W) & (lane1 < TOK_W + N_SEQ) & (least > SLOT - 0.5)
    full = jnp.min(jnp.where(is_full, lane1f, 1e9), axis=1, keepdims=True)

    def first_row(r, w):
        return jnp.sum(jnp.where(lane1f == full + N_SEQ, ids[r, w], 0.0), axis=1, keepdims=True)

    lane = lax.broadcasted_iota(jnp.int32, (TOK_W, 128), 1)
    tok = lax.broadcasted_iota(jnp.int32, (TOK_W, 128), 0)

    def column(row):
        return jnp.sum(jnp.where(lane == tok, row, 0.0), axis=1, keepdims=True)

    FOUR = 4 * TOK_W
    r4 = lax.broadcasted_iota(jnp.int32, (FOUR, 1), 0)
    c4 = lax.broadcasted_iota(jnp.int32, (FOUR, FOUR), 1).astype(F32)
    who4, place4 = (r4 >> 5) & 3, ((r4 >> 7) * SLOT + (r4 & (SLOT - 1))).astype(F32)

    def sort_keys(r):
        for u in range(2):
            begin = jnp.zeros((FOUR, 1), F32)
            parts = []
            for n in range(4):
                w = 4 * u + n
                begin = jnp.where(who4 == n, first_row(r, w), begin)
                hot = (lane.astype(F32) == column(ids[r, w])) | (lane == 32 + r * N_HEAD + w)
                parts.append(jnp.where(hot, 1.0, 0.0).astype(BF16))
            t = begin + place4
            t = jnp.where(t >= TOK_W, t - TOK_W, t) + (who4 * TOK_W).astype(F32)
            move = jnp.where(c4 == t, 1.0, 0.0).astype(BF16)
            rows = pl.ds(pl.multiple_of(r * ROW + u * FOUR, FOUR), FOUR)
            both = jnp.dot(move, kv[rows, :], preferred_element_type=F32).astype(BF16)
            marks = jnp.dot(move, jnp.concatenate(parts, axis=0), preferred_element_type=F32).astype(BF16)
            here = pl.ds(u * 128, 128)
            for f in range(2):
                ks[f, r, here, 0:HEAD_SIZE] = both[f * 128 : (f + 1) * 128, 0:HEAD_SIZE]
                ks[f, r, here, HEAD_SIZE:] = marks[f * 128 : (f + 1) * 128]
                vs[f, r, here, :] = both[f * 128 : (f + 1) * 128, HEAD_SIZE:]

    c1 = lax.broadcasted_iota(jnp.int32, (TOK_W, TOK_W), 1).astype(F32)
    r1 = lax.broadcasted_iota(jnp.int32, (TOK_W, TOK_W), 0).astype(F32)

    def prepare_queries(p, carry):
        w = z * N_HEAD + p
        b = w // 4
        c = column(ids[z, p])
        shard = jnp.floor(c * 0.25)
        looks = jnp.zeros((TOK_W, 128), F32)
        for s in range(N_SEQ):
            looks = jnp.where(shard == float(s), anc[s, b], looks)
        worker = lane - 32
        own_block = ((worker >> 2) == b) & (worker <= w)
        fine = jnp.where(
            lane < 32,
            jnp.where(lane.astype(F32) == c, 1.0, 0.0),
            jnp.where((lane >= 96) | own_block, 1.0, looks),
        )
        penalty = jnp.where(fine > 0.5, 0.0, NEG).astype(BF16)
        t = first_row(z, p) + r1
        t = jnp.where(t >= TOK_W, t - TOK_W, t)
        move = jnp.where(c1 == t, 1.0, 0.0).astype(BF16)
        rows = jnp.dot(move, qbuf[p], preferred_element_type=F32).astype(BF16)
        marks = jnp.dot(move, penalty, preferred_element_type=F32).astype(BF16)
        for f in range(2):
            part = slice(f * SLOT, (f + 1) * SLOT)
            for g in range(GROUP):
                to = pl.ds(pl.multiple_of(p * TILE + g * SLOT, SLOT), SLOT)
                qa[f, to, 0:HEAD_SIZE] = rows[part, g * HEAD_SIZE : (g + 1) * HEAD_SIZE]
                qa[f, to, HEAD_SIZE:] = marks[part]
        return carry

    BLOCK = 512
    row_id = lax.broadcasted_iota(jnp.int32, (BLOCK, HALF), 0)
    col_id = lax.broadcasted_iota(jnp.int32, (BLOCK, HALF), 1)
    late_pos = (col_id & (SLOT - 1)) > (row_id & (SLOT - 1))

    def score(r, f, is_own):
        def block(n, carry):
            at = pl.ds(pl.multiple_of(n * BLOCK, BLOCK), BLOCK)
            s = lax.dot_general(qa[f, at, :], ks[f, r], NT, preferred_element_type=F32) * FACTOR
            if is_own:
                late = late_pos & ((col_id >> 5) == (row_id >> 8) + n * (BLOCK // TILE))
                s = jnp.where(late, NEG, s)
            sbuf[f, r, at, :] = s
            top = jnp.maximum(s[:, 0:128], s[:, 128:])
            mx[f, at, :] = top if is_own else jnp.maximum(mx[f, at, :], top)
            return carry

        lax.fori_loop(0, QROWS // BLOCK, block, 0)

    def sort_if(r):
        @pl.when(r <= z)
        def _():
            sort_keys(r)

    def score_if(r):
        @pl.when(r <= z)
        def _():
            for f in range(2):
                score(r, f, False)

    def forward(t, j):
        for way in range(2):
            if (way, t - 1, j) in ring:
                ring[way, t - 1, j].wait_recv()
            if (way, t, j) in ring:
                ring[way, t, j].start()

    def ready_queries():
        own[2].wait()
        for c in q_row:
            c.wait_recv()
        lax.fori_loop(0, N_HEAD, prepare_queries, 0)

    near = {(way, t): source(way, t) for way in range(2) for t in range(1, 4)}
    opposite = lax.rem(z + 4, N_SEQ)
    sort_keys(z)
    for j in range(4):
        forward(1, j)
    forward(2, 0)
    sort_if(near[0, 1])
    forward(2, 1)
    sort_if(near[1, 1])
    forward(2, 2)
    forward(2, 3)
    ready_queries()
    forward(3, 0)
    forward(3, 1)
    sort_if(near[0, 2])
    score(z, 0, True)
    score(z, 1, True)
    forward(3, 2)
    forward(3, 3)
    sort_if(near[1, 2])
    for way in range(2):
        score_if(near[way, 1])
        score_if(near[way, 2])
    sort_if(near[0, 3])
    sort_if(near[1, 3])
    for way in range(2):
        score_if(near[way, 3])
    for j in range(4):
        forward(4, j)
    sort_if(opposite)
    score_if(opposite)

    def tile(d, carry):
        p = lax.rem(h + d, N_HEAD)
        at = pl.ds(pl.multiple_of(p * TILE, TILE), TILE)
        for f in range(2):
            top = jnp.max(mx[f, at, :], axis=1, keepdims=True)
            mx[f, at, :] = jnp.broadcast_to(top, (TILE, 128))
            den[f] = jnp.zeros((TILE, 128), F32)
            acc[f] = jnp.zeros((TILE, HEAD_SIZE), F32)

        def blend(i, carry):
            for f in range(2):
                top = mx[f, at, :]
                weights = jnp.exp2(sbuf[f, i, at, :] - jnp.concatenate([top, top], axis=1))
                den[f] += weights[:, 0:128] + weights[:, 128:]
                acc[f] += jnp.dot(weights.astype(BF16), vs[f, i], preferred_element_type=F32)
            return carry

        lax.fori_loop(0, z + 1, blend, 0)
        for f in range(2):
            total = jnp.sum(den[f], axis=1, keepdims=True)
            done = (acc[f] / total).astype(BF16)
            for g in range(GROUP):
                osort[f * SLOT : (f + 1) * SLOT, g * HEAD_SIZE : (g + 1) * HEAD_SIZE] = done[
                    g * SLOT : (g + 1) * SLOT
                ]
        t = r1 - first_row(z, p)
        t = jnp.where(t < 0.0, t + TOK_W, t)
        back = jnp.where(c1 == t, 1.0, 0.0).astype(BF16)
        stage[p] = jnp.dot(back, osort[...], preferred_element_type=F32).astype(BF16)

        @pl.when(d < N_HEAD)
        def _():
            remote(stage.at[p], out_ref.at[:, wide(h)], o_s.at[d], o_r.at[d], head=p).start()

        return carry

    lax.fori_loop(1, N_HEAD + 1, tile, 0)
    last = pltpu.make_async_copy(stage.at[h], out_ref.at[:, wide(h)], own_sem.at[0])
    last.start()
    last.wait()
    for c in id_row + k_row + v_row + q_row + id_col + an_col + list(ring.values()):
        c.wait_send()
    for d in range(1, N_HEAD):
        p = lax.rem(h + d, N_HEAD)
        remote(stage.at[p], out_ref.at[:, wide(h)], o_s.at[d], o_r.at[d], head=p).wait()


def body(queries, keys, values, counts, offsets, tree_ids, block_lists):
    any_space = pl.BlockSpec(memory_space=pl.ANY)
    smem = pl.BlockSpec(memory_space=pltpu.SMEM)
    dma = pltpu.SemaphoreType.DMA
    return pl.pallas_call(
        kernel,
        out_shape=jax.ShapeDtypeStruct((TOK_W, KEY_VALUE_HEADS * WIDE), BF16),
        in_specs=[smem] * 4 + [any_space] * 3,
        out_specs=any_space,
        scratch_shapes=[
            pltpu.VMEM((N_HEAD, TOK_W, WIDE), BF16),
            pltpu.VMEM((N_SEQ * ROW, 2 * HEAD_SIZE), BF16),
            pltpu.VMEM((2, N_SEQ, HALF, 2 * HEAD_SIZE), BF16),
            pltpu.VMEM((2, N_SEQ, HALF, HEAD_SIZE), BF16),
            pltpu.VMEM((N_SEQ, N_HEAD, 1, 128), F32),
            pltpu.VMEM((N_SEQ, QB, 1, 128), F32),
            pltpu.VMEM((2, QROWS, 2 * HEAD_SIZE), BF16),
            pltpu.VMEM((2, N_SEQ, QROWS, HALF), F32),
            pltpu.VMEM((2, QROWS, 128), F32),
            pltpu.VMEM((2, TILE, 128), F32),
            pltpu.VMEM((2, TILE, HEAD_SIZE), F32),
            pltpu.VMEM((TOK_W, WIDE), BF16),
            pltpu.VMEM((N_HEAD, TOK_W, WIDE), BF16),
            dma((3,)),
            dma((N_HEAD, 2)),
            dma((N_HEAD, 2)),
            dma((N_HEAD,)),
            dma((N_HEAD,)),
            dma((N_HEAD,)),
            dma((N_HEAD,)),
            dma((2, 4, 4)),
            dma((2, 4, 4)),
            dma((N_SEQ,)),
            dma((N_SEQ,)),
            dma((N_SEQ,)),
            dma((N_SEQ,)),
            dma((N_HEAD + 1,)),
            dma((N_HEAD + 1,)),
        ],
        compiler_params=pltpu.CompilerParams(
            collective_id=0, has_side_effects=True, vmem_limit_bytes=62 * 1024 * 1024
        ),
    )(counts, offsets, tree_ids, jnp.transpose(block_lists, (2, 0, 1)), queries, keys, values)


def solution(mesh):
    split = P(("rep", "seq", "head"), None)
    placed = (split,) * 6 + (P(("rep", "seq"), None, None),)
    return jax.shard_map(body, mesh=mesh, in_specs=placed, out_specs=split, check_vma=False)
```

time: 96.8 us -> 72.1 us (0.74)
  the two profiles are of different devices: /device:TPU:240 before, /device:TPU:235 now
where the time goes in v2:
time: 72.1 us; the launch traced here: 72 us
  Pallas kernels  69.7 us (97%)
  local copies, waits for them, and re-layouts  2.26 us (3%)
    pallas_call x1, Pallas kernels, body(): pl.pallas_call(kernel, out_shape=jax.ShapeDtypeStruct((TOK_W, KEY_VALUE_H...  69.7 us
    unnamed x1, local copies, waits for them, and re-layouts  2.26 us

profile of v2, /device:TPU:235, one launch (start us, length us, event | category | flops | bytes accessed | tf_op | source)
XLA Modules:
  0.0 72.0 jit_solution(6273063323241473254)
XLA Ops:
  0.0 69.7 %shard_map.73 = bf16[64,8192]{1,0:T(8,128)(2,1)} custom-call(s32[1,8]{1,0:T(1,128)} %cnt_ref.1, s32[1,8]{1,0:T(1,128)} %off_ref.1, s32[1,8]{1,0:T(1,128)} %tree_ref.1, s32[7,1,16]{2,1,0:T(1,128)} %bitcast.1, bf16[64,8192]{1,0:T(8,128)(2,1)} %q_ref.1, bf16[64,1024]{1,0:T(8,128)(2,1)} %k_ref.1, bf16[64,1024]{1,0:T(8,128)(2,1)} %v_ref.1), custom_call_target="tpu_custom_call" | custom-call | tf_op jit(solution)/shard_map/pallas_call | solution.py:365
  69.7 2.3 %copy.9 = bf16[64,8192]{1,0:T(8,128)(2,1)} copy(bf16[64,8192]{1,0:T(8,128)(2,1)} %shard_map.73) | data formatting | bytes 2097152

commit v3 on v2

--- a/solution.py
+++ b/solution.py
@@ -1,3 +1,4 @@
+import functools
 import math
 
 import jax
@@ -33,7 +34,7 @@
 
 def kernel(
     cnt_ref, off_ref, tree_ref, bl_ref, q_ref, k_ref, v_ref, out_ref,
-    qbuf, kv, ks, vs, ids, anc, qa, sbuf, mx, den, acc, osort, stage,
+    qbuf, kv, ks, vs, ids, anc, qa, sbuf, mx, osort, stage,
     own_sem, kv_s, kv_r, id_s, id_r, q_s, q_r, ring_s, ring_r, idr_s, idr_r, an_s, an_r, o_s, o_r,
 ):
     z = lax.axis_index("seq")
@@ -202,7 +203,7 @@
             for f in range(2):
                 ks[f, r, here, 0:HEAD_SIZE] = both[f * 128 : (f + 1) * 128, 0:HEAD_SIZE]
                 ks[f, r, here, HEAD_SIZE:] = marks[f * 128 : (f + 1) * 128]
-                vs[f, r, here, :] = both[f * 128 : (f + 1) * 128, HEAD_SIZE:]
+                vs[f, pl.ds(pl.multiple_of(r * HALF + u * 128, 128), 128), :] = both[f * 128 : (f + 1) * 128, HEAD_SIZE:]
 
     c1 = lax.broadcasted_iota(jnp.int32, (TOK_W, TOK_W), 1).astype(F32)
     r1 = lax.broadcasted_iota(jnp.int32, (TOK_W, TOK_W), 0).astype(F32)
@@ -236,7 +237,7 @@
                 qa[f, to, HEAD_SIZE:] = marks[part]
         return carry
 
-    BLOCK = 512
+    BLOCK = 2048
     row_id = lax.broadcasted_iota(jnp.int32, (BLOCK, HALF), 0)
     col_id = lax.broadcasted_iota(jnp.int32, (BLOCK, HALF), 1)
     late_pos = (col_id & (SLOT - 1)) > (row_id & (SLOT - 1))
@@ -248,7 +249,7 @@
             if is_own:
                 late = late_pos & ((col_id >> 5) == (row_id >> 8) + n * (BLOCK // TILE))
                 s = jnp.where(late, NEG, s)
-            sbuf[f, r, at, :] = s
+            sbuf[f, at, pl.ds(pl.multiple_of(r * HALF, HALF), HALF)] = s
             top = jnp.maximum(s[:, 0:128], s[:, 128:])
             mx[f, at, :] = top if is_own else jnp.maximum(mx[f, at, :], top)
             return carry
@@ -256,12 +257,12 @@
         lax.fori_loop(0, QROWS // BLOCK, block, 0)
 
     def sort_if(r):
-        @pl.when(r <= z)
+        @pl.when(r < bound)
         def _():
             sort_keys(r)
 
     def score_if(r):
-        @pl.when(r <= z)
+        @pl.when(r < bound)
         def _():
             for f in range(2):
                 score(r, f, False)
@@ -279,6 +280,7 @@
             c.wait_recv()
         lax.fori_loop(0, N_HEAD, prepare_queries, 0)
 
+    bound = jnp.where(z < N_SEQ // 2, N_SEQ // 2, N_SEQ)
     near = {(way, t): source(way, t) for way in range(2) for t in range(1, 4)}
     opposite = lax.rem(z + 4, N_SEQ)
     sort_keys(z)
@@ -290,48 +292,41 @@
     sort_if(near[1, 1])
     forward(2, 2)
     forward(2, 3)
+    forward(3, 0)
+    sort_if(near[0, 2])
+    forward(3, 1)
+    sort_if(near[1, 2])
     ready_queries()
-    forward(3, 0)
-    forward(3, 1)
-    sort_if(near[0, 2])
+    forward(3, 2)
     score(z, 0, True)
     score(z, 1, True)
-    forward(3, 2)
     forward(3, 3)
-    sort_if(near[1, 2])
+    score_if(near[0, 1])
+    score_if(near[1, 1])
+    forward(4, 0)
+    forward(4, 2)
+    score_if(near[0, 2])
+    score_if(near[1, 2])
     for way in range(2):
-        score_if(near[way, 1])
-        score_if(near[way, 2])
-    sort_if(near[0, 3])
-    sort_if(near[1, 3])
-    for way in range(2):
+        sort_if(near[way, 3])
         score_if(near[way, 3])
-    for j in range(4):
-        forward(4, j)
+    forward(4, 1)
+    forward(4, 3)
     sort_if(opposite)
     score_if(opposite)
 
-    def tile(d, carry):
+    def tile(limit, d, carry):
         p = lax.rem(h + d, N_HEAD)
         at = pl.ds(pl.multiple_of(p * TILE, TILE), TILE)
+        keys = limit * HALF
         for f in range(2):
-            top = jnp.max(mx[f, at, :], axis=1, keepdims=True)
-            mx[f, at, :] = jnp.broadcast_to(top, (TILE, 128))
-            den[f] = jnp.zeros((TILE, 128), F32)
-            acc[f] = jnp.zeros((TILE, HEAD_SIZE), F32)
-
-        def blend(i, carry):
-            for f in range(2):
-                top = mx[f, at, :]
-                weights = jnp.exp2(sbuf[f, i, at, :] - jnp.concatenate([top, top], axis=1))
-                den[f] += weights[:, 0:128] + weights[:, 128:]
-                acc[f] += jnp.dot(weights.astype(BF16), vs[f, i], preferred_element_type=F32)
-            return carry
-
-        lax.fori_loop(0, z + 1, blend, 0)
-        for f in range(2):
-            total = jnp.sum(den[f], axis=1, keepdims=True)
-            done = (acc[f] / total).astype(BF16)
+            top = jnp.broadcast_to(jnp.max(mx[f, at, :], axis=1, keepdims=True), (TILE, 128))
+            weights = jnp.exp2(sbuf[f, at, 0:keys] - jnp.concatenate([top] * (keys // 128), axis=1))
+            total = weights[:, 0:128]
+            for n in range(1, keys // 128):
+                total = total + weights[:, n * 128 : (n + 1) * 128]
+            blend = jnp.dot(weights.astype(BF16), vs[f, 0:keys, :], preferred_element_type=F32)
+            done = (blend / jnp.sum(total, axis=1, keepdims=True)).astype(BF16)
             for g in range(GROUP):
                 osort[f * SLOT : (f + 1) * SLOT, g * HEAD_SIZE : (g + 1) * HEAD_SIZE] = done[
                     g * SLOT : (g + 1) * SLOT
@@ -347,7 +342,12 @@
 
         return carry
 
-    lax.fori_loop(1, N_HEAD + 1, tile, 0)
+    for limit in (N_SEQ // 2, N_SEQ):
+
+        @pl.when(bound == limit)
+        def _():
+            lax.fori_loop(1, N_HEAD + 1, functools.partial(tile, limit), 0)
+
     last = pltpu.make_async_copy(stage.at[h], out_ref.at[:, wide(h)], own_sem.at[0])
     last.start()
     last.wait()
@@ -371,14 +371,12 @@
             pltpu.VMEM((N_HEAD, TOK_W, WIDE), BF16),
             pltpu.VMEM((N_SEQ * ROW, 2 * HEAD_SIZE), BF16),
             pltpu.VMEM((2, N_SEQ, HALF, 2 * HEAD_SIZE), BF16),
-            pltpu.VMEM((2, N_SEQ, HALF, HEAD_SIZE), BF16),
+            pltpu.VMEM((2, N_SEQ * HALF, HEAD_SIZE), BF16),
             pltpu.VMEM((N_SEQ, N_HEAD, 1, 128), F32),
             pltpu.VMEM((N_SEQ, QB, 1, 128), F32),
             pltpu.VMEM((2, QROWS, 2 * HEAD_SIZE), BF16),
-            pltpu.VMEM((2, N_SEQ, QROWS, HALF), F32),
+            pltpu.VMEM((2, QROWS, N_SEQ * HALF), F32),
             pltpu.VMEM((2, QROWS, 128), F32),
-            pltpu.VMEM((2, TILE, 128), F32),
-            pltpu.VMEM((2, TILE, HEAD_SIZE), F32),
             pltpu.VMEM((TOK_W, WIDE), BF16),
             pltpu.VMEM((N_HEAD, TOK_W, WIDE), BF16),
             dma((3,)),

time: 72.1 us -> 60.4 us (0.84)
  Pallas kernels: 69.7 us -> 58 us
    pallas_call x1, Pallas kernels: 69.7 us -> 58 us  [body(): pl.pallas_call(kernel, out_shape=jax.ShapeDtypeStruct((TOK_W, KEY_VALUE_H...]
where the time goes in v3:
time: 60.4 us; the launch traced here: 60.3 us
  Pallas kernels  58 us (96%)
  local copies, waits for them, and re-layouts  2.26 us (4%)
    pallas_call x1, Pallas kernels, body(): pl.pallas_call(kernel, out_shape=jax.ShapeDtypeStruct((TOK_W, KEY_VALUE_H...  58 us
    unnamed x1, local copies, waits for them, and re-layouts  2.26 us

profile of v3, /device:TPU:235, one launch (start us, length us, event | category | flops | bytes accessed | tf_op | source)
XLA Modules:
  0.0 60.3 jit_solution(16851396937605468568)
XLA Ops:
  0.0 58.0 %shard_map.73 = bf16[64,8192]{1,0:T(8,128)(2,1)} custom-call(s32[1,8]{1,0:T(1,128)} %cnt_ref.1, s32[1,8]{1,0:T(1,128)} %off_ref.1, s32[1,8]{1,0:T(1,128)} %tree_ref.1, s32[7,1,16]{2,1,0:T(1,128)} %bitcast.1, bf16[64,8192]{1,0:T(8,128)(2,1)} %q_ref.1, bf16[64,1024]{1,0:T(8,128)(2,1)} %k_ref.1, bf16[64,1024]{1,0:T(8,128)(2,1)} %v_ref.1), custom_call_target="tpu_custom_call" | custom-call | tf_op jit(solution)/shard_map/pallas_call | solution.py:365
  58.0 2.3 %copy.9 = bf16[64,8192]{1,0:T(8,128)(2,1)} copy(bf16[64,8192]{1,0:T(8,128)(2,1)} %shard_map.73) | data formatting | bytes 2097152

commit v4 on v3

--- a/solution.py
+++ b/solution.py
@@ -23,6 +23,7 @@
 WIDE = GROUP * HEAD_SIZE
 TILE = GROUP * SLOT
 QROWS = N_HEAD * TILE
+FOUR = 4 * TOK_W
 PIECE = 2 * TOK_W
 ORDER = (0, 1, 3, 2)
 NEG = -1e30
@@ -34,7 +35,7 @@
 
 def kernel(
     cnt_ref, off_ref, tree_ref, bl_ref, q_ref, k_ref, v_ref, out_ref,
-    qbuf, kv, ks, vs, ids, anc, qa, sbuf, mx, osort, stage,
+    qbuf, kv, ks, vs, moves, turns, ids, anc, qa, sbuf, mx, osort, stage,
     own_sem, kv_s, kv_r, id_s, id_r, q_s, q_r, ring_s, ring_r, idr_s, idr_r, an_s, an_r, o_s, o_r,
 ):
     z = lax.axis_index("seq")
@@ -145,21 +146,28 @@
         landed(j)
         for way in range(2):
             ring[way, 0, j].start()
-        if j == 0:
-            for c in q_row:
-                c.start()
-        if j == 1:
-            for c in id_row:
-                c.wait_recv()
-            id_col, an_col = [], []
-            for e in range(1, N_SEQ):
-                to = lax.rem(z + e, N_SEQ)
-                id_col.append(remote(ids.at[z], ids.at[z], idr_s.at[e], idr_r.at[e], seq=to))
-                two = pl.ds(2 * to, 2)
-                an_col.append(remote(anc.at[z, two], anc.at[z, two], an_s.at[e], an_r.at[e], seq=to))
-            for c in id_col + an_col:
-                c.start()
-
+    for c in q_row:
+        c.start()
+    for c in id_row:
+        c.wait_recv()
+    id_col, an_col = [], []
+    for e in range(1, N_SEQ):
+        to = lax.rem(z + e, N_SEQ)
+        id_col.append(remote(ids.at[z], ids.at[z], idr_s.at[e], idr_r.at[e], seq=to))
+        two = pl.ds(2 * to, 2)
+        an_col.append(remote(anc.at[z, two], anc.at[z, two], an_s.at[e], an_r.at[e], seq=to))
+    for c in id_col + an_col:
+        c.start()
+
+    def forward(t, j):
+        for way in range(2):
+            if (way, t - 1, j) in ring:
+                ring[way, t - 1, j].wait_recv()
+            if (way, t, j) in ring:
+                ring[way, t, j].start()
+
+    forward(1, 0)
+    forward(1, 1)
     for c in id_col + an_col:
         c.wait_recv()
     least = jnp.full((1, 128), 1e9, F32)
@@ -179,36 +187,40 @@
     def column(row):
         return jnp.sum(jnp.where(lane == tok, row, 0.0), axis=1, keepdims=True)
 
-    FOUR = 4 * TOK_W
     r4 = lax.broadcasted_iota(jnp.int32, (FOUR, 1), 0)
     c4 = lax.broadcasted_iota(jnp.int32, (FOUR, FOUR), 1).astype(F32)
     who4, place4 = (r4 >> 5) & 3, ((r4 >> 7) * SLOT + (r4 & (SLOT - 1))).astype(F32)
 
-    def sort_keys(r):
+    def mark_keys(r):
         for u in range(2):
-            begin = jnp.zeros((FOUR, 1), F32)
+            first = jnp.zeros((FOUR, 1), F32)
             parts = []
             for n in range(4):
                 w = 4 * u + n
-                begin = jnp.where(who4 == n, first_row(r, w), begin)
+                first = jnp.where(who4 == n, first_row(r, w), first)
                 hot = (lane.astype(F32) == column(ids[r, w])) | (lane == 32 + r * N_HEAD + w)
                 parts.append(jnp.where(hot, 1.0, 0.0).astype(BF16))
-            t = begin + place4
+            t = first + place4
             t = jnp.where(t >= TOK_W, t - TOK_W, t) + (who4 * TOK_W).astype(F32)
             move = jnp.where(c4 == t, 1.0, 0.0).astype(BF16)
+            moves[r, u] = move
+            marks = jnp.dot(move, jnp.concatenate(parts, axis=0), preferred_element_type=F32).astype(BF16)
+            for f in range(2):
+                ks[f, r, u * 128 : (u + 1) * 128, HEAD_SIZE:] = marks[f * 128 : (f + 1) * 128]
+
+    def sort_keys(r):
+        for u in range(2):
             rows = pl.ds(pl.multiple_of(r * ROW + u * FOUR, FOUR), FOUR)
-            both = jnp.dot(move, kv[rows, :], preferred_element_type=F32).astype(BF16)
-            marks = jnp.dot(move, jnp.concatenate(parts, axis=0), preferred_element_type=F32).astype(BF16)
-            here = pl.ds(u * 128, 128)
+            both = jnp.dot(moves[r, u], kv[rows, :], preferred_element_type=F32).astype(BF16)
             for f in range(2):
-                ks[f, r, here, 0:HEAD_SIZE] = both[f * 128 : (f + 1) * 128, 0:HEAD_SIZE]
-                ks[f, r, here, HEAD_SIZE:] = marks[f * 128 : (f + 1) * 128]
-                vs[f, pl.ds(pl.multiple_of(r * HALF + u * 128, 128), 128), :] = both[f * 128 : (f + 1) * 128, HEAD_SIZE:]
+                part = slice(f * 128, (f + 1) * 128)
+                ks[f, r, u * 128 : (u + 1) * 128, 0:HEAD_SIZE] = both[part, 0:HEAD_SIZE]
+                vs[f, pl.ds(pl.multiple_of(r * HALF + u * 128, 128), 128), :] = both[part, HEAD_SIZE:]
 
     c1 = lax.broadcasted_iota(jnp.int32, (TOK_W, TOK_W), 1).astype(F32)
     r1 = lax.broadcasted_iota(jnp.int32, (TOK_W, TOK_W), 0).astype(F32)
 
-    def prepare_queries(p, carry):
+    def mark_queries(p, carry):
         w = z * N_HEAD + p
         b = w // 4
         c = column(ids[z, p])
@@ -227,14 +239,22 @@
         t = first_row(z, p) + r1
         t = jnp.where(t >= TOK_W, t - TOK_W, t)
         move = jnp.where(c1 == t, 1.0, 0.0).astype(BF16)
-        rows = jnp.dot(move, qbuf[p], preferred_element_type=F32).astype(BF16)
+        turns[p] = move
         marks = jnp.dot(move, penalty, preferred_element_type=F32).astype(BF16)
         for f in range(2):
             part = slice(f * SLOT, (f + 1) * SLOT)
             for g in range(GROUP):
                 to = pl.ds(pl.multiple_of(p * TILE + g * SLOT, SLOT), SLOT)
+                qa[f, to, HEAD_SIZE:] = marks[part]
+        return carry
+
+    def sort_queries(p, carry):
+        rows = jnp.dot(turns[p], qbuf[p], preferred_element_type=F32).astype(BF16)
+        for f in range(2):
+            part = slice(f * SLOT, (f + 1) * SLOT)
+            for g in range(GROUP):
+                to = pl.ds(pl.multiple_of(p * TILE + g * SLOT, SLOT), SLOT)
                 qa[f, to, 0:HEAD_SIZE] = rows[part, g * HEAD_SIZE : (g + 1) * HEAD_SIZE]
-                qa[f, to, HEAD_SIZE:] = marks[part]
         return carry
 
     BLOCK = 2048
@@ -267,56 +287,64 @@
             for f in range(2):
                 score(r, f, False)
 
-    def forward(t, j):
-        for way in range(2):
-            if (way, t - 1, j) in ring:
-                ring[way, t - 1, j].wait_recv()
-            if (way, t, j) in ring:
-                ring[way, t, j].start()
-
     def ready_queries():
         own[2].wait()
         for c in q_row:
             c.wait_recv()
-        lax.fori_loop(0, N_HEAD, prepare_queries, 0)
+        lax.fori_loop(0, N_HEAD, sort_queries, 0)
 
     bound = jnp.where(z < N_SEQ // 2, N_SEQ // 2, N_SEQ)
     near = {(way, t): source(way, t) for way in range(2) for t in range(1, 4)}
     opposite = lax.rem(z + 4, N_SEQ)
+    def mark_if(r):
+        @pl.when(r < bound)
+        def _():
+            mark_keys(r)
+
+    forward(1, 2)
+    forward(1, 3)
+    mark_keys(z)
     sort_keys(z)
-    for j in range(4):
-        forward(1, j)
     forward(2, 0)
-    sort_if(near[0, 1])
     forward(2, 1)
-    sort_if(near[1, 1])
+    mark_if(near[0, 1])
+    mark_if(near[1, 1])
     forward(2, 2)
     forward(2, 3)
+    sort_if(near[0, 1])
+    sort_if(near[1, 1])
+    lax.fori_loop(0, N_HEAD, mark_queries, 0)
+    mark_if(near[0, 2])
     forward(3, 0)
+    forward(3, 1)
+    mark_if(near[1, 2])
+    mark_if(near[0, 3])
+    forward(3, 2)
+    forward(3, 3)
+    mark_if(near[1, 3])
+    mark_if(opposite)
     sort_if(near[0, 2])
-    forward(3, 1)
     sort_if(near[1, 2])
     ready_queries()
-    forward(3, 2)
     score(z, 0, True)
     score(z, 1, True)
-    forward(3, 3)
-    score_if(near[0, 1])
-    score_if(near[1, 1])
-    forward(4, 0)
-    forward(4, 2)
-    score_if(near[0, 2])
-    score_if(near[1, 2])
+    for way in range(2):
+        score_if(near[way, 1])
+        score_if(near[way, 2])
     for way in range(2):
         sort_if(near[way, 3])
         score_if(near[way, 3])
-    forward(4, 1)
-    forward(4, 3)
+    for j in range(4):
+        forward(4, j)
     sort_if(opposite)
     score_if(opposite)
 
-    def tile(limit, d, carry):
-        p = lax.rem(h + d, N_HEAD)
+    def tile(limit, step, carry):
+        m = lax.rem(step, 3)
+        across = jnp.where(step < 6, 2 - m + 3 * (m // 2), 0)
+        other = jnp.where(step < 6, step // 3, 7 - step)
+        p = lax.rem(h // 2 + across, 4) * 2 + lax.rem(h + other, 2)
+        d = lax.rem(p - h + N_HEAD, N_HEAD)
         at = pl.ds(pl.multiple_of(p * TILE, TILE), TILE)
         keys = limit * HALF
         for f in range(2):
@@ -336,7 +364,7 @@
         back = jnp.where(c1 == t, 1.0, 0.0).astype(BF16)
         stage[p] = jnp.dot(back, osort[...], preferred_element_type=F32).astype(BF16)
 
-        @pl.when(d < N_HEAD)
+        @pl.when(p != h)
         def _():
             remote(stage.at[p], out_ref.at[:, wide(h)], o_s.at[d], o_r.at[d], head=p).start()
 
@@ -346,7 +374,7 @@
 
         @pl.when(bound == limit)
         def _():
-            lax.fori_loop(1, N_HEAD + 1, functools.partial(tile, limit), 0)
+            lax.fori_loop(0, N_HEAD, functools.partial(tile, limit), 0)
 
     last = pltpu.make_async_copy(stage.at[h], out_ref.at[:, wide(h)], own_sem.at[0])
     last.start()
@@ -365,13 +393,15 @@
     return pl.pallas_call(
         kernel,
         out_shape=jax.ShapeDtypeStruct((TOK_W, KEY_VALUE_HEADS * WIDE), BF16),
-        in_specs=[smem] * 4 + [any_space] * 3,
+        in_specs=[smem] * 4 + [pl.BlockSpec(memory_space=pltpu.HBM)] * 3,
         out_specs=any_space,
         scratch_shapes=[
             pltpu.VMEM((N_HEAD, TOK_W, WIDE), BF16),
             pltpu.VMEM((N_SEQ * ROW, 2 * HEAD_SIZE), BF16),
             pltpu.VMEM((2, N_SEQ, HALF, 2 * HEAD_SIZE), BF16),
             pltpu.VMEM((2, N_SEQ * HALF, HEAD_SIZE), BF16),
+            pltpu.VMEM((N_SEQ, 2, FOUR, FOUR), BF16),
+            pltpu.VMEM((N_HEAD, TOK_W, TOK_W), BF16),
             pltpu.VMEM((N_SEQ, N_HEAD, 1, 128), F32),
             pltpu.VMEM((N_SEQ, QB, 1, 128), F32),
             pltpu.VMEM((2, QROWS, 2 * HEAD_SIZE), BF16),
@@ -396,7 +426,7 @@
             dma((N_HEAD + 1,)),
         ],
         compiler_params=pltpu.CompilerParams(
-            collective_id=0, has_side_effects=True, vmem_limit_bytes=62 * 1024 * 1024
+            collective_id=0, has_side_effects=True, vmem_limit_bytes=58 * 1024 * 1024
         ),
     )(counts, offsets, tree_ids, jnp.transpose(block_lists, (2, 0, 1)), queries, keys, values)
 

time: 60.4 us -> 57.4 us (0.950); the launches traced: 60.3 us -> 56.6 us
  Pallas kernels: 58 us -> 54.4 us
    pallas_call x1, Pallas kernels: 58 us -> 54.4 us  [body(): pl.pallas_call(kernel, out_shape=jax.ShapeDtypeStruct((TOK_W, KEY_VALUE_H...]
where the time goes in v4:
time: 57.4 us; the launch traced here: 56.6 us
  Pallas kernels  54.4 us (95%)
  local copies, waits for them, and re-layouts  2.26 us (4%)
    pallas_call x1, Pallas kernels, body(): pl.pallas_call(kernel, out_shape=jax.ShapeDtypeStruct((TOK_W, KEY_VALUE_H...  54.4 us
    unnamed x1, local copies, waits for them, and re-layouts  2.26 us

profile of v4, /device:TPU:235, one launch (start us, length us, event | category | flops | bytes accessed | tf_op | source)
XLA Modules:
  0.0 56.6 jit_solution(14018900651626407959)
XLA Ops:
  0.0 54.4 %shard_map.73 = bf16[64,8192]{1,0:T(8,128)(2,1)} custom-call(s32[1,8]{1,0:T(1,128)} %cnt_ref.1, s32[1,8]{1,0:T(1,128)} %off_ref.1, s32[1,8]{1,0:T(1,128)} %tree_ref.1, s32[7,1,16]{2,1,0:T(1,128)} %bitcast.1, bf16[64,8192]{1,0:T(8,128)(2,1)} %q_ref.1, bf16[64,1024]{1,0:T(8,128)(2,1)} %k_ref.1, bf16[64,1024]{1,0:T(8,128)(2,1)} %v_ref.1), custom_call_target="tpu_custom_call" | custom-call | tf_op jit(solution)/shard_map/pallas_call | solution.py:393
  54.4 2.3 %copy.9 = bf16[64,8192]{1,0:T(8,128)(2,1)} copy(bf16[64,8192]{1,0:T(8,128)(2,1)} %shard_map.73) | data formatting | bytes 2097152

commit v5 on v4

--- a/solution.py
+++ b/solution.py
@@ -89,25 +89,30 @@
             src_ref=src, dst_ref=dst, send_sem=s_sem, recv_sem=r_sem, device_id=where, device_id_type=MESH
         )
 
-    others = [lax.rem(h + d, N_HEAD) for d in range(N_HEAD)]
-    id_row = [remote(ids.at[z, h], ids.at[z, h], id_s.at[d], id_r.at[d], head=others[d]) for d in range(1, N_HEAD)]
+    core = lax.rem(h, 2)
+    others = [
+        lax.rem(h // 2 + across, 4) * 2 + lax.rem(core + other, 2)
+        for across, other in ((0, 1), (1, 0), (3, 0), (1, 1), (3, 1), (2, 0), (2, 1))
+    ]
+    apart = [lax.rem(p - h + N_HEAD, N_HEAD) for p in others]
+    id_row = [remote(ids.at[z, h], ids.at[z, h], id_s.at[d], id_r.at[d], head=p) for p, d in zip(others, apart)]
     k_row = [
-        remote(k_ref.at[:, cols(others[d])], kv.at[mine, left], kv_s.at[d, 0], kv_r.at[d, 0], head=others[d])
-        for d in range(1, N_HEAD)
+        remote(k_ref.at[:, cols(p)], kv.at[mine, left], kv_s.at[d, 0], kv_r.at[d, 0], head=p)
+        for p, d in zip(others, apart)
     ]
     v_row = [
-        remote(v_ref.at[:, cols(others[d])], kv.at[mine, right], kv_s.at[d, 1], kv_r.at[d, 1], head=others[d])
-        for d in range(1, N_HEAD)
+        remote(v_ref.at[:, cols(p)], kv.at[mine, right], kv_s.at[d, 1], kv_r.at[d, 1], head=p)
+        for p, d in zip(others, apart)
     ]
     q_row = [
-        remote(q_ref.at[:, wide(others[d])], qbuf.at[h], q_s.at[d], q_r.at[d], head=others[d])
-        for d in range(1, N_HEAD)
+        remote(q_ref.at[:, wide(p)], qbuf.at[h], q_s.at[d], q_r.at[d], head=p)
+        for p, d in zip(others, apart)
     ]
-    for c in id_row:
-        c.start()
     for a, b in zip(k_row, v_row):
         a.start()
         b.start()
+    for c in id_row:
+        c.start()
 
     chip = h // 2
 
@@ -220,7 +225,7 @@
     c1 = lax.broadcasted_iota(jnp.int32, (TOK_W, TOK_W), 1).astype(F32)
     r1 = lax.broadcasted_iota(jnp.int32, (TOK_W, TOK_W), 0).astype(F32)
 
-    def mark_queries(p, carry):
+    def mark_queries(p):
         w = z * N_HEAD + p
         b = w // 4
         c = column(ids[z, p])
@@ -244,18 +249,16 @@
         for f in range(2):
             part = slice(f * SLOT, (f + 1) * SLOT)
             for g in range(GROUP):
-                to = pl.ds(pl.multiple_of(p * TILE + g * SLOT, SLOT), SLOT)
+                to = pl.ds(p * TILE + g * SLOT, SLOT)
                 qa[f, to, HEAD_SIZE:] = marks[part]
-        return carry
-
-    def sort_queries(p, carry):
+
+    def sort_queries(p):
         rows = jnp.dot(turns[p], qbuf[p], preferred_element_type=F32).astype(BF16)
         for f in range(2):
             part = slice(f * SLOT, (f + 1) * SLOT)
             for g in range(GROUP):
-                to = pl.ds(pl.multiple_of(p * TILE + g * SLOT, SLOT), SLOT)
+                to = pl.ds(p * TILE + g * SLOT, SLOT)
                 qa[f, to, 0:HEAD_SIZE] = rows[part, g * HEAD_SIZE : (g + 1) * HEAD_SIZE]
-        return carry
 
     BLOCK = 2048
     row_id = lax.broadcasted_iota(jnp.int32, (BLOCK, HALF), 0)
@@ -291,7 +294,8 @@
         own[2].wait()
         for c in q_row:
             c.wait_recv()
-        lax.fori_loop(0, N_HEAD, sort_queries, 0)
+        for p in range(N_HEAD):
+            sort_queries(p)
 
     bound = jnp.where(z < N_SEQ // 2, N_SEQ // 2, N_SEQ)
     near = {(way, t): source(way, t) for way in range(2) for t in range(1, 4)}
@@ -302,27 +306,30 @@
             mark_keys(r)
 
     forward(1, 2)
+    mark_keys(z)
     forward(1, 3)
-    mark_keys(z)
+    mark_if(near[0, 1])
+    forward(2, 0)
+    mark_if(near[1, 1])
+    forward(2, 1)
+    mark_if(near[0, 2])
+    forward(2, 2)
+    mark_if(near[1, 2])
+    forward(2, 3)
+    mark_if(near[0, 3])
+    for p in range(N_HEAD // 2):
+        mark_queries(p)
+    forward(3, 0)
+    mark_if(near[1, 3])
+    for p in range(N_HEAD // 2, N_HEAD):
+        mark_queries(p)
+    forward(3, 1)
+    mark_if(opposite)
     sort_keys(z)
-    forward(2, 0)
-    forward(2, 1)
-    mark_if(near[0, 1])
-    mark_if(near[1, 1])
-    forward(2, 2)
-    forward(2, 3)
+    forward(3, 2)
     sort_if(near[0, 1])
     sort_if(near[1, 1])
-    lax.fori_loop(0, N_HEAD, mark_queries, 0)
-    mark_if(near[0, 2])
-    forward(3, 0)
-    forward(3, 1)
-    mark_if(near[1, 2])
-    mark_if(near[0, 3])
-    forward(3, 2)
     forward(3, 3)
-    mark_if(near[1, 3])
-    mark_if(opposite)
     sort_if(near[0, 2])
     sort_if(near[1, 2])
     ready_queries()
@@ -331,11 +338,13 @@
     for way in range(2):
         score_if(near[way, 1])
         score_if(near[way, 2])
+    forward(4, 0)
+    forward(4, 2)
     for way in range(2):
         sort_if(near[way, 3])
         score_if(near[way, 3])
-    for j in range(4):
-        forward(4, j)
+    forward(4, 1)
+    forward(4, 3)
     sort_if(opposite)
     score_if(opposite)
 

time: 57.4 us -> 55.1 us (0.960)
  the two profiles are of different devices: /device:TPU:235 before, /device:TPU:1 now
where the time goes in v5:
time: 55.1 us; the launch traced here: 55 us
  Pallas kernels  52.7 us (96%)
  local copies, waits for them, and re-layouts  2.26 us (4%)
    pallas_call x1, Pallas kernels, body(): pl.pallas_call(kernel, out_shape=jax.ShapeDtypeStruct((TOK_W, KEY_VALUE_H...  52.7 us
    unnamed x1, local copies, waits for them, and re-layouts  2.26 us

profile of v5, /device:TPU:1, one launch (start us, length us, event | category | flops | bytes accessed | tf_op | source)
XLA Modules:
  0.0 55.0 jit_solution(561806104812669632)
XLA Ops:
  0.0 52.7 %shard_map.73 = bf16[64,8192]{1,0:T(8,128)(2,1)} custom-call(s32[1,8]{1,0:T(1,128)} %cnt_ref.1, s32[1,8]{1,0:T(1,128)} %off_ref.1, s32[1,8]{1,0:T(1,128)} %tree_ref.1, s32[7,1,16]{2,1,0:T(1,128)} %bitcast.1, bf16[64,8192]{1,0:T(8,128)(2,1)} %q_ref.1, bf16[64,1024]{1,0:T(8,128)(2,1)} %k_ref.1, bf16[64,1024]{1,0:T(8,128)(2,1)} %v_ref.1), custom_call_target="tpu_custom_call" | custom-call | tf_op jit(solution)/shard_map/pallas_call | solution.py:402
  52.7 2.3 %copy.9 = bf16[64,8192]{1,0:T(8,128)(2,1)} copy(bf16[64,8192]{1,0:T(8,128)(2,1)} %shard_map.73) | data formatting | bytes 2097152

commit v6 on v5

--- a/solution.py
+++ b/solution.py
@@ -132,6 +132,12 @@
 
     ring = {(way, t, j): hop(way, t, j) for way in range(2) for t in range(4) for j in pieces(way, t)}
 
+    def goes(way, t):
+        return (z < N_SEQ - 1) & (z >= t) if way == 0 else source(1, t) < N_SEQ // 2
+
+    def comes(way, t):
+        return z > t if way == 0 else lax.rem(z + 1 + t, N_SEQ) < N_SEQ // 2
+
     def landed(j):
         for q in range(2):
             src = lax.rem(chip + ORDER[j], 4) * 2 + q
@@ -150,7 +156,11 @@
     for j in range(4):
         landed(j)
         for way in range(2):
-            ring[way, 0, j].start()
+
+            @pl.when(goes(way, 0))
+            def _():
+                ring[way, 0, j].start()
+
     for c in q_row:
         c.start()
     for c in id_row:
@@ -167,9 +177,17 @@
     def forward(t, j):
         for way in range(2):
             if (way, t - 1, j) in ring:
-                ring[way, t - 1, j].wait_recv()
+
+                @pl.when(comes(way, t - 1))
+                def _():
+                    ring[way, t - 1, j].wait_recv()
+
             if (way, t, j) in ring:
-                ring[way, t, j].start()
+
+                @pl.when(goes(way, t))
+                def _():
+                    ring[way, t, j].start()
+
 
     forward(1, 0)
     forward(1, 1)
@@ -280,9 +298,15 @@
         lax.fori_loop(0, QROWS // BLOCK, block, 0)
 
     def sort_if(r):
-        @pl.when(r < bound)
+        @pl.when(r <= z)
         def _():
             sort_keys(r)
+
+        @pl.when((r > z) & (r < bound))
+        def _():
+            for f in range(2):
+                ks[f, r, :, 0:HEAD_SIZE] = jnp.zeros((HALF, HEAD_SIZE), BF16)
+                vs[f, pl.ds(pl.multiple_of(r * HALF, HALF), HALF), :] = jnp.zeros((HALF, HEAD_SIZE), BF16)
 
     def score_if(r):
         @pl.when(r < bound)
@@ -388,8 +412,14 @@
     last = pltpu.make_async_copy(stage.at[h], out_ref.at[:, wide(h)], own_sem.at[0])
     last.start()
     last.wait()
-    for c in id_row + k_row + v_row + q_row + id_col + an_col + list(ring.values()):
+    for c in id_row + k_row + v_row + q_row + id_col + an_col:
         c.wait_send()
+    for (way, t, j), c in ring.items():
+
+        @pl.when(goes(way, t))
+        def _():
+            c.wait_send()
+
     for d in range(1, N_HEAD):
         p = lax.rem(h + d, N_HEAD)
         remote(stage.at[p], out_ref.at[:, wide(h)], o_s.at[d], o_r.at[d], head=p).wait()

time: 55.1 us -> 54.5 us (0.989)
  the two profiles are of different devices: /device:TPU:1 before, /device:TPU:235 now
where the time goes in v6:
time: 54.5 us; the launch traced here: 53.6 us
  Pallas kernels  51.3 us (94%)
  local copies, waits for them, and re-layouts  2.26 us (4%)
    pallas_call x1, Pallas kernels, body(): pl.pallas_call(kernel, out_shape=jax.ShapeDtypeStruct((TOK_W, KEY_VALUE_H...  51.3 us
    unnamed x1, local copies, waits for them, and re-layouts  2.26 us

profile of v6, /device:TPU:235, one launch (start us, length us, event | category | flops | bytes accessed | tf_op | source)
XLA Modules:
  0.0 53.6 jit_solution(14227848147631899690)
XLA Ops:
  0.0 51.3 %shard_map.73 = bf16[64,8192]{1,0:T(8,128)(2,1)} custom-call(s32[1,8]{1,0:T(1,128)} %cnt_ref.1, s32[1,8]{1,0:T(1,128)} %off_ref.1, s32[1,8]{1,0:T(1,128)} %tree_ref.1, s32[7,1,16]{2,1,0:T(1,128)} %bitcast.1, bf16[64,8192]{1,0:T(8,128)(2,1)} %q_ref.1, bf16[64,1024]{1,0:T(8,128)(2,1)} %k_ref.1, bf16[64,1024]{1,0:T(8,128)(2,1)} %v_ref.1), custom_call_target="tpu_custom_call" | custom-call | tf_op jit(solution)/shard_map/pallas_call | solution.py:432
  51.3 2.3 %copy.9 = bf16[64,8192]{1,0:T(8,128)(2,1)} copy(bf16[64,8192]{1,0:T(8,128)(2,1)} %shard_map.73) | data formatting | bytes 2097152
